TPU v7x, 32 devices: a whole 2x2x4 slice. The times are simulated.
32 devices in a mesh: section: 4 (over y, core), dp: 8 (over z, x).
Axes of the slice: x: 2, y: 2, z: 4, core: 2. Of those that a mesh axis runs over, the one named last changes fastest.
Arguments:
- token_states: bfloat16 [4, 128, 8192], P(None, 'dp'), may hold values from -10 to 10
- norm_gains: float32 [4, 8192], P('section'), may hold values from 1 to 4
- prompt_kv: bfloat16 [4, 1024, 2048], P('section'), may hold values from -11 to 11
- history_kv: bfloat16 [4, 128, 28, 2048], P('section', 'dp'), may hold values from -6 to 6
- new_kv: bfloat16 [4, 4, 128, 2048], P('section', None, 'dp'), may hold values from -6 to 6
- ancestors: int32 [128], replicated, may hold values from 0 to 127, as said below
Outputs:
- attention_out: bfloat16 [4, 4, 128, 8192], P('section', None, 'dp')
- forked_kv: bfloat16 [4, 128, 32, 2048], P('section', 'dp')
Inputs may be any that keep to these rules, and one draw needn't show every extreme that they name: Of the 16 ancestors of particles p * 16 .. p * 16 + 15, at most one distinct value lies in any block q * 16 .. q * 16 + 15; ancestors may repeat.
All inputs are finite; a program needn't handle non-finite values.
Results may differ from a plain program's by a relative error of at most 0.0086.
Values may be sent and summed in bfloat16 or wider, within the bound.
A program may use at most 128 MiB of HBM per device.

v0:
```python
import jax
import jax.numpy as jnp
from jax import lax
from jax.sharding import PartitionSpec as P

HEADS = 64
KV_HEADS = 8
HEAD_DIM = 128


NEG_FILL = -1e30


def passed_along(block, axis, distance):
    devices = range(lax.axis_size(axis))
    route = [((i - distance) % len(devices), i) for i in devices]
    return lax.ppermute(block, axis, route)


def normalize(values):
    return values * lax.rsqrt(jnp.mean(values * values, axis=-1, keepdims=True) + 1e-05)


def attend(hidden, gains_row, prompt, history, recent, step_now):
    rows = hidden.shape[0]
    half = KV_HEADS * HEAD_DIM
    share = HEADS // KV_HEADS
    queries = (
        (normalize(hidden) * gains_row)
        .astype(jnp.bfloat16)
        .reshape(rows, KV_HEADS, share, HEAD_DIM)
    )
    prompt_keys = prompt[:, :half].reshape(-1, KV_HEADS, HEAD_DIM)
    prompt_vals = prompt[:, half:].reshape(-1, KV_HEADS, HEAD_DIM)
    past_keys = history[..., :half].reshape(rows, -1, KV_HEADS, HEAD_DIM)
    past_vals = history[..., half:].reshape(rows, -1, KV_HEADS, HEAD_DIM)
    recent_keys = recent[..., :half].reshape(-1, rows, KV_HEADS, HEAD_DIM)
    recent_vals = recent[..., half:].reshape(-1, rows, KV_HEADS, HEAD_DIM)
    score_scale = HEAD_DIM ** (-0.5)
    prompt_scores = (
        jnp.einsum("pkgd,nkd->pkgn", queries, prompt_keys, preferred_element_type=jnp.float32)
        * score_scale
    )
    past_scores = (
        jnp.einsum("pkgd,pnkd->pkgn", queries, past_keys, preferred_element_type=jnp.float32)
        * score_scale
    )
    recent_scores = (
        jnp.einsum("pkgd,npkd->pkgn", queries, recent_keys, preferred_element_type=jnp.float32)
        * score_scale
    )
    present = jnp.arange(recent.shape[0]) <= step_now
    recent_scores = jnp.where(present, recent_scores, NEG_FILL)
    highest = jnp.maximum(
        jnp.max(prompt_scores, -1, keepdims=True), jnp.max(past_scores, -1, keepdims=True)
    )
    highest = jnp.maximum(highest, jnp.max(recent_scores, -1, keepdims=True))
    prompt_exp = jnp.exp(prompt_scores - highest)
    past_exp = jnp.exp(past_scores - highest)
    recent_exp = jnp.exp(recent_scores - highest)
    denominator = (
        jnp.sum(prompt_exp, -1, keepdims=True)
        + jnp.sum(past_exp, -1, keepdims=True)
        + jnp.sum(recent_exp, -1, keepdims=True)
    )
    mixed = jnp.einsum(
        "pkgn,nkd->pkgd",
        (prompt_exp / denominator).astype(jnp.bfloat16),
        prompt_vals,
        preferred_element_type=jnp.float32,
    )
    mixed = mixed + jnp.einsum(
        "pkgn,pnkd->pkgd",
        (past_exp / denominator).astype(jnp.bfloat16),
        past_vals,
        preferred_element_type=jnp.float32,
    )
    mixed = mixed + jnp.einsum(
        "pkgn,npkd->pkgd",
        (recent_exp / denominator).astype(jnp.bfloat16),
        recent_vals,
        preferred_element_type=jnp.float32,
    )
    return mixed.reshape(rows, HEADS * HEAD_DIM)


def fork_cache(history, recent, ancestors, part_dev):
    shards = lax.axis_size("dp")
    own_index = lax.axis_index("dp")
    particle_cache = jnp.concatenate([history, jnp.transpose(recent, (1, 0, 2))], axis=1)
    owners = ancestors.reshape(shards, part_dev)
    picked = jnp.max(jnp.where(owners // part_dev == own_index, owners % part_dev, 0), axis=1)
    outgoing = jnp.take(particle_cache, picked, axis=0)
    incoming = lax.all_to_all(outgoing, "dp", split_axis=0, concat_axis=0, tiled=True)
    own_ancestors = lax.dynamic_slice_in_dim(ancestors, own_index * part_dev, part_dev)
    return jnp.take(incoming, own_ancestors // part_dev, axis=0)[None]


def local(token_states, norm_gains, prompt_kv, history_kv, new_kv, ancestors):
    section_count = lax.axis_size("section")
    section_index = lax.axis_index("section")
    part_dev = history_kv.shape[1]
    steps = new_kv.shape[1]
    model_width = token_states.shape[2]
    gains_row = norm_gains[0]
    prompt = prompt_kv[0]
    history = history_kv[0]
    recent = new_kv[0]
    groups = 1
    group_rows = part_dev // groups
    moments = steps * section_count + groups - 1

    def advance(moment, carry):
        arrived, outbuf = carry
        offset = moment - section_index
        step_raw = jnp.floor_divide(offset, section_count)
        group_raw = jnp.mod(offset, section_count)
        active = (offset >= 0) & (step_raw < steps) & (group_raw < groups)
        step_now = jnp.clip(step_raw, 0, steps - 1)
        group_now = jnp.clip(group_raw, 0, groups - 1)
        start = group_now * group_rows
        zero = jnp.zeros((), jnp.int32)
        token_rows = lax.dynamic_slice(
            token_states, (step_now, start, zero), (1, group_rows, model_width)
        )[0].astype(jnp.float32)
        carried = jnp.where(step_now > 0, normalize(arrived), 0.0)
        hidden = jnp.where(section_index == 0, token_rows + carried, arrived)
        mixed = attend(hidden, gains_row, prompt, history, recent, step_now)
        previous = lax.dynamic_slice(outbuf, (step_now, start, zero), (1, group_rows, model_width))
        written = jnp.where(active, mixed.astype(jnp.bfloat16)[None], previous)
        outbuf = lax.dynamic_update_slice(outbuf, written, (step_now, start, zero))
        passed = passed_along(hidden + mixed, "section", 1)
        return (passed, outbuf)

    start_carry = (
        jnp.zeros((group_rows, model_width), jnp.float32),
        jnp.zeros((steps, part_dev, model_width), jnp.bfloat16),
    )
    arrived, outbuf = lax.fori_loop(0, moments, advance, start_carry)
    forked_kv = fork_cache(history, recent, ancestors, part_dev)
    return (outbuf[None], forked_kv)


def solution(mesh):
    in_specs = (
        P(None, "dp", None),
        P("section", None),
        P("section", None, None),
        P("section", "dp", None, None),
        P("section", None, "dp", None),
        P(),
    )
    out_specs = (P("section", None, "dp", None), P("section", "dp", None, None))
    return jax.shard_map(local, mesh=mesh, in_specs=in_specs, out_specs=out_specs, check_vma=False)
```

profile of v0, /device:TPU:5, one launch (start us, length us, event | category | flops | bytes accessed | tf_op | source)
XLA Modules:
  0.0 785.2 jit_solution(6845482789107358479)
XLA Ops:
  7.4 5.5 all-to-all-start
  12.9 6.4 copy.118
  20.3 17.2 %all-to-all-done = bf16[8,32,2048]{2,1,0:T(8,128)(2,1)S(1)} async-done(((bf16[8,32,2048]{2,1,0:T(8,128)(2,1)}), bf16[8,32,2048]{2,1,0:T(8,128)(2,1)S(1)}, u32[]{:S(2)}, u32[]{:S(2)}) %all-to-all-start) | async-done | bytes 1048608 | tf_op jit(solution)/shard_map/all_to_all | solution.py:94
  39.5 3.3 bitcast_select_fusion
  43.9 741.3 %while.17 = (s32[]{:T(128)}, f32[16,8192]{1,0:T(8,128)S(1)}, bf16[4,16,8192]{2,1,0:T(8,128)(2,1)}, pred[]{:T(512)}, s32[]{:T(128)}, /*index=5*/bf16[4,16,8192]{2...) while((s32[]{:T(128)}, f32[16,8192]{1,0:T(8,128)S(1)}, ...), condition=%wide.region_9.10_spmd, body=%wide.region_0.9_spmd.sunk | while | flops 566855744 | bytes 67499304 | solution.py:139
  50.0 4.1 fusion.63
  63.7 3.7 fusion.67
  86.7 3.2 collective-permute-done
  96.1 4.1 fusion.63
  109.8 3.7 fusion.67
  133.1 3.2 collective-permute-done
  142.4 4.1 fusion.63
  156.1 3.7 fusion.67
  179.4 3.2 collective-permute-done
  188.8 4.1 fusion.63
  202.5 3.7 fusion.67
  225.8 3.2 collective-permute-done
  235.1 4.1 fusion.63
  248.8 3.7 fusion.67
  272.1 3.2 collective-permute-done
  281.5 4.1 fusion.63
  295.2 3.7 fusion.67
  318.5 3.2 collective-permute-done
  327.8 4.1 fusion.63
  341.5 3.7 fusion.67
  364.8 3.2 collective-permute-done
  374.2 4.1 fusion.63
  387.9 3.7 fusion.67
  411.2 3.2 collective-permute-done
  420.5 4.1 fusion.63
  434.2 3.7 fusion.67
  457.5 3.2 collective-permute-done
  466.9 4.1 fusion.63
  480.6 3.7 fusion.67
  503.9 3.2 collective-permute-done
  513.2 4.1 fusion.63
  526.9 3.7 fusion.67
  550.2 3.2 collective-permute-done
  559.6 4.1 fusion.63
  573.3 3.7 fusion.67
  605.9 4.1 fusion.63
  619.6 3.7 fusion.67
  652.3 4.1 fusion.63
  666.0 3.7 fusion.67
  698.6 4.1 fusion.63
  712.3 3.7 fusion.67
  745.0 4.1 fusion.63
  758.7 3.7 fusion.67
  (873 shorter events, 589.6 us)
Async XLA Ops:
  7.4 30.1 %all-to-all-start = ((bf16[8,32,2048]{2,1,0:T(8,128)(2,1)}), bf16[8,32,2048]{2,1,0:T(8,128)(2,1)S(1)}, u32[]{:S(2)}, u32[]{:S(2)}) async-start(bf16[8,32,2048]{2,1,0:T(8,128)(2,1)} %broadcast_select_fusion), calls=%async_computation | async-start | bytes 2097152 | tf_op jit(solution)/shard_map/all_to_all | solution.py:94
  12.9 7.3 copy-start.8
  61.8 5.6 copy-start.4
  63.7 9.6 %copy-start.3 = (bf16[4,16,1024]{2,1,0:T(8,128)(2,1)S(1)}, bf16[4,16,1024]{2,1,0:T(8,128)(2,1)}, u32[]{:S(2)}) copy-start(bf16[4,16,1024]{2,1,0:T(8,128)(2,1)} %get-tuple-element.385) | copy-start | bytes 393220 | tf_op jit(solution)/shard_map/while
  81.6 8.4 %collective-permute-start = (f32[16,8192]{1,0:T(8,128)S(1)}, f32[16,8192]{1,0:T(8,128)S(1)}, u32[]{:S(2)}, u32[]{:S(2)}) collective-permute-start(f32[16,8192]{1,0:T(8,128)S(1)} %bitcast_add_fusion.2), channel_id=1, source_target_pairs={{24,0},{0,8},{8,16},{16,24},{25,1},{1,9},{9,17},{17,25},{26,2},{2,... | collective-permute-start | bytes 1572872 | tf_op jit(solution)/shard_map/while/body/eval_jaxpr/ppermute | solution.py:17
  107.9 5.6 copy-start.4
  109.8 9.6 %copy-start.3 = (bf16[4,16,1024]{2,1,0:T(8,128)(2,1)S(1)}, bf16[4,16,1024]{2,1,0:T(8,128)(2,1)}, u32[]{:S(2)}) copy-start(bf16[4,16,1024]{2,1,0:T(8,128)(2,1)} %get-tuple-element.385) | copy-start | bytes 393220 | tf_op jit(solution)/shard_map/while
  127.7 8.7 %collective-permute-start = (f32[16,8192]{1,0:T(8,128)S(1)}, f32[16,8192]{1,0:T(8,128)S(1)}, u32[]{:S(2)}, u32[]{:S(2)}) collective-permute-start(f32[16,8192]{1,0:T(8,128)S(1)} %bitcast_add_fusion.2), channel_id=1, source_target_pairs={{24,0},{0,8},{8,16},{16,24},{25,1},{1,9},{9,17},{17,25},{26,2},{2,... | collective-permute-start | bytes 1572872 | tf_op jit(solution)/shard_map/while/body/eval_jaxpr/ppermute | solution.py:17
  154.2 5.6 copy-start.4
  156.1 9.6 %copy-start.3 = (bf16[4,16,1024]{2,1,0:T(8,128)(2,1)S(1)}, bf16[4,16,1024]{2,1,0:T(8,128)(2,1)}, u32[]{:S(2)}) copy-start(bf16[4,16,1024]{2,1,0:T(8,128)(2,1)} %get-tuple-element.385) | copy-start | bytes 393220 | tf_op jit(solution)/shard_map/while
  174.0 8.7 %collective-permute-start = (f32[16,8192]{1,0:T(8,128)S(1)}, f32[16,8192]{1,0:T(8,128)S(1)}, u32[]{:S(2)}, u32[]{:S(2)}) collective-permute-start(f32[16,8192]{1,0:T(8,128)S(1)} %bitcast_add_fusion.2), channel_id=1, source_target_pairs={{24,0},{0,8},{8,16},{16,24},{25,1},{1,9},{9,17},{17,25},{26,2},{2,... | collective-permute-start | bytes 1572872 | tf_op jit(solution)/shard_map/while/body/eval_jaxpr/ppermute | solution.py:17
  200.6 5.6 copy-start.4
  202.5 9.6 %copy-start.3 = (bf16[4,16,1024]{2,1,0:T(8,128)(2,1)S(1)}, bf16[4,16,1024]{2,1,0:T(8,128)(2,1)}, u32[]{:S(2)}) copy-start(bf16[4,16,1024]{2,1,0:T(8,128)(2,1)} %get-tuple-element.385) | copy-start | bytes 393220 | tf_op jit(solution)/shard_map/while
  220.4 8.7 %collective-permute-start = (f32[16,8192]{1,0:T(8,128)S(1)}, f32[16,8192]{1,0:T(8,128)S(1)}, u32[]{:S(2)}, u32[]{:S(2)}) collective-permute-start(f32[16,8192]{1,0:T(8,128)S(1)} %bitcast_add_fusion.2), channel_id=1, source_target_pairs={{24,0},{0,8},{8,16},{16,24},{25,1},{1,9},{9,17},{17,25},{26,2},{2,... | collective-permute-start | bytes 1572872 | tf_op jit(solution)/shard_map/while/body/eval_jaxpr/ppermute | solution.py:17
  246.9 5.6 copy-start.4
  248.8 9.6 %copy-start.3 = (bf16[4,16,1024]{2,1,0:T(8,128)(2,1)S(1)}, bf16[4,16,1024]{2,1,0:T(8,128)(2,1)}, u32[]{:S(2)}) copy-start(bf16[4,16,1024]{2,1,0:T(8,128)(2,1)} %get-tuple-element.385) | copy-start | bytes 393220 | tf_op jit(solution)/shard_map/while
  266.7 8.7 %collective-permute-start = (f32[16,8192]{1,0:T(8,128)S(1)}, f32[16,8192]{1,0:T(8,128)S(1)}, u32[]{:S(2)}, u32[]{:S(2)}) collective-permute-start(f32[16,8192]{1,0:T(8,128)S(1)} %bitcast_add_fusion.2), channel_id=1, source_target_pairs={{24,0},{0,8},{8,16},{16,24},{25,1},{1,9},{9,17},{17,25},{26,2},{2,... | collective-permute-start | bytes 1572872 | tf_op jit(solution)/shard_map/while/body/eval_jaxpr/ppermute | solution.py:17
  293.3 5.6 copy-start.4
  295.2 9.6 %copy-start.3 = (bf16[4,16,1024]{2,1,0:T(8,128)(2,1)S(1)}, bf16[4,16,1024]{2,1,0:T(8,128)(2,1)}, u32[]{:S(2)}) copy-start(bf16[4,16,1024]{2,1,0:T(8,128)(2,1)} %get-tuple-element.385) | copy-start | bytes 393220 | tf_op jit(solution)/shard_map/while
  313.1 8.7 %collective-permute-start = (f32[16,8192]{1,0:T(8,128)S(1)}, f32[16,8192]{1,0:T(8,128)S(1)}, u32[]{:S(2)}, u32[]{:S(2)}) collective-permute-start(f32[16,8192]{1,0:T(8,128)S(1)} %bitcast_add_fusion.2), channel_id=1, source_target_pairs={{24,0},{0,8},{8,16},{16,24},{25,1},{1,9},{9,17},{17,25},{26,2},{2,... | collective-permute-start | bytes 1572872 | tf_op jit(solution)/shard_map/while/body/eval_jaxpr/ppermute | solution.py:17
  339.6 5.6 copy-start.4
  341.5 9.6 %copy-start.3 = (bf16[4,16,1024]{2,1,0:T(8,128)(2,1)S(1)}, bf16[4,16,1024]{2,1,0:T(8,128)(2,1)}, u32[]{:S(2)}) copy-start(bf16[4,16,1024]{2,1,0:T(8,128)(2,1)} %get-tuple-element.385) | copy-start | bytes 393220 | tf_op jit(solution)/shard_map/while
  359.4 8.7 %collective-permute-start = (f32[16,8192]{1,0:T(8,128)S(1)}, f32[16,8192]{1,0:T(8,128)S(1)}, u32[]{:S(2)}, u32[]{:S(2)}) collective-permute-start(f32[16,8192]{1,0:T(8,128)S(1)} %bitcast_add_fusion.2), channel_id=1, source_target_pairs={{24,0},{0,8},{8,16},{16,24},{25,1},{1,9},{9,17},{17,25},{26,2},{2,... | collective-permute-start | bytes 1572872 | tf_op jit(solution)/shard_map/while/body/eval_jaxpr/ppermute | solution.py:17
  386.0 5.6 copy-start.4
  387.9 9.6 %copy-start.3 = (bf16[4,16,1024]{2,1,0:T(8,128)(2,1)S(1)}, bf16[4,16,1024]{2,1,0:T(8,128)(2,1)}, u32[]{:S(2)}) copy-start(bf16[4,16,1024]{2,1,0:T(8,128)(2,1)} %get-tuple-element.385) | copy-start | bytes 393220 | tf_op jit(solution)/shard_map/while
  405.8 8.7 %collective-permute-start = (f32[16,8192]{1,0:T(8,128)S(1)}, f32[16,8192]{1,0:T(8,128)S(1)}, u32[]{:S(2)}, u32[]{:S(2)}) collective-permute-start(f32[16,8192]{1,0:T(8,128)S(1)} %bitcast_add_fusion.2), channel_id=1, source_target_pairs={{24,0},{0,8},{8,16},{16,24},{25,1},{1,9},{9,17},{17,25},{26,2},{2,... | collective-permute-start | bytes 1572872 | tf_op jit(solution)/shard_map/while/body/eval_jaxpr/ppermute | solution.py:17
  432.3 5.6 copy-start.4
  434.2 9.6 %copy-start.3 = (bf16[4,16,1024]{2,1,0:T(8,128)(2,1)S(1)}, bf16[4,16,1024]{2,1,0:T(8,128)(2,1)}, u32[]{:S(2)}) copy-start(bf16[4,16,1024]{2,1,0:T(8,128)(2,1)} %get-tuple-element.385) | copy-start | bytes 393220 | tf_op jit(solution)/shard_map/while
  452.1 8.7 %collective-permute-start = (f32[16,8192]{1,0:T(8,128)S(1)}, f32[16,8192]{1,0:T(8,128)S(1)}, u32[]{:S(2)}, u32[]{:S(2)}) collective-permute-start(f32[16,8192]{1,0:T(8,128)S(1)} %bitcast_add_fusion.2), channel_id=1, source_target_pairs={{24,0},{0,8},{8,16},{16,24},{25,1},{1,9},{9,17},{17,25},{26,2},{2,... | collective-permute-start | bytes 1572872 | tf_op jit(solution)/shard_map/while/body/eval_jaxpr/ppermute | solution.py:17
  478.7 5.6 copy-start.4
  480.6 9.6 %copy-start.3 = (bf16[4,16,1024]{2,1,0:T(8,128)(2,1)S(1)}, bf16[4,16,1024]{2,1,0:T(8,128)(2,1)}, u32[]{:S(2)}) copy-start(bf16[4,16,1024]{2,1,0:T(8,128)(2,1)} %get-tuple-element.385) | copy-start | bytes 393220 | tf_op jit(solution)/shard_map/while
  498.5 8.7 %collective-permute-start = (f32[16,8192]{1,0:T(8,128)S(1)}, f32[16,8192]{1,0:T(8,128)S(1)}, u32[]{:S(2)}, u32[]{:S(2)}) collective-permute-start(f32[16,8192]{1,0:T(8,128)S(1)} %bitcast_add_fusion.2), channel_id=1, source_target_pairs={{24,0},{0,8},{8,16},{16,24},{25,1},{1,9},{9,17},{17,25},{26,2},{2,... | collective-permute-start | bytes 1572872 | tf_op jit(solution)/shard_map/while/body/eval_jaxpr/ppermute | solution.py:17
  525.0 5.6 copy-start.4
  526.9 9.6 %copy-start.3 = (bf16[4,16,1024]{2,1,0:T(8,128)(2,1)S(1)}, bf16[4,16,1024]{2,1,0:T(8,128)(2,1)}, u32[]{:S(2)}) copy-start(bf16[4,16,1024]{2,1,0:T(8,128)(2,1)} %get-tuple-element.385) | copy-start | bytes 393220 | tf_op jit(solution)/shard_map/while
  544.8 8.7 %collective-permute-start = (f32[16,8192]{1,0:T(8,128)S(1)}, f32[16,8192]{1,0:T(8,128)S(1)}, u32[]{:S(2)}, u32[]{:S(2)}) collective-permute-start(f32[16,8192]{1,0:T(8,128)S(1)} %bitcast_add_fusion.2), channel_id=1, source_target_pairs={{24,0},{0,8},{8,16},{16,24},{25,1},{1,9},{9,17},{17,25},{26,2},{2,... | collective-permute-start | bytes 1572872 | tf_op jit(solution)/shard_map/while/body/eval_jaxpr/ppermute | solution.py:17
  571.4 5.6 copy-start.4
  573.3 9.6 %copy-start.3 = (bf16[4,16,1024]{2,1,0:T(8,128)(2,1)S(1)}, bf16[4,16,1024]{2,1,0:T(8,128)(2,1)}, u32[]{:S(2)}) copy-start(bf16[4,16,1024]{2,1,0:T(8,128)(2,1)} %get-tuple-element.385) | copy-start | bytes 393220 | tf_op jit(solution)/shard_map/while
  591.2 8.7 %collective-permute-start = (f32[16,8192]{1,0:T(8,128)S(1)}, f32[16,8192]{1,0:T(8,128)S(1)}, u32[]{:S(2)}, u32[]{:S(2)}) collective-permute-start(f32[16,8192]{1,0:T(8,128)S(1)} %bitcast_add_fusion.2), channel_id=1, source_target_pairs={{24,0},{0,8},{8,16},{16,24},{25,1},{1,9},{9,17},{17,25},{26,2},{2,... | collective-permute-start | bytes 1572872 | tf_op jit(solution)/shard_map/while/body/eval_jaxpr/ppermute | solution.py:17
  617.7 5.6 copy-start.4
  619.6 9.6 %copy-start.3 = (bf16[4,16,1024]{2,1,0:T(8,128)(2,1)S(1)}, bf16[4,16,1024]{2,1,0:T(8,128)(2,1)}, u32[]{:S(2)}) copy-start(bf16[4,16,1024]{2,1,0:T(8,128)(2,1)} %get-tuple-element.385) | copy-start | bytes 393220 | tf_op jit(solution)/shard_map/while
  637.5 8.7 %collective-permute-start = (f32[16,8192]{1,0:T(8,128)S(1)}, f32[16,8192]{1,0:T(8,128)S(1)}, u32[]{:S(2)}, u32[]{:S(2)}) collective-permute-start(f32[16,8192]{1,0:T(8,128)S(1)} %bitcast_add_fusion.2), channel_id=1, source_target_pairs={{24,0},{0,8},{8,16},{16,24},{25,1},{1,9},{9,17},{17,25},{26,2},{2,... | collective-permute-start | bytes 1572872 | tf_op jit(solution)/shard_map/while/body/eval_jaxpr/ppermute | solution.py:17
  664.1 5.6 copy-start.4
  666.0 9.6 %copy-start.3 = (bf16[4,16,1024]{2,1,0:T(8,128)(2,1)S(1)}, bf16[4,16,1024]{2,1,0:T(8,128)(2,1)}, u32[]{:S(2)}) copy-start(bf16[4,16,1024]{2,1,0:T(8,128)(2,1)} %get-tuple-element.385) | copy-start | bytes 393220 | tf_op jit(solution)/shard_map/while
  683.9 8.7 %collective-permute-start = (f32[16,8192]{1,0:T(8,128)S(1)}, f32[16,8192]{1,0:T(8,128)S(1)}, u32[]{:S(2)}, u32[]{:S(2)}) collective-permute-start(f32[16,8192]{1,0:T(8,128)S(1)} %bitcast_add_fusion.2), channel_id=1, source_target_pairs={{24,0},{0,8},{8,16},{16,24},{25,1},{1,9},{9,17},{17,25},{26,2},{2,... | collective-permute-start | bytes 1572872 | tf_op jit(solution)/shard_map/while/body/eval_jaxpr/ppermute | solution.py:17
  712.3 9.6 %copy-start.3 = (bf16[4,16,1024]{2,1,0:T(8,128)(2,1)S(1)}, bf16[4,16,1024]{2,1,0:T(8,128)(2,1)}, u32[]{:S(2)}) copy-start(bf16[4,16,1024]{2,1,0:T(8,128)(2,1)} %get-tuple-element.385) | copy-start | bytes 393220 | tf_op jit(solution)/shard_map/while
  730.2 8.7 %collective-permute-start = (f32[16,8192]{1,0:T(8,128)S(1)}, f32[16,8192]{1,0:T(8,128)S(1)}, u32[]{:S(2)}, u32[]{:S(2)}) collective-permute-start(f32[16,8192]{1,0:T(8,128)S(1)} %bitcast_add_fusion.2), channel_id=1, source_target_pairs={{24,0},{0,8},{8,16},{16,24},{25,1},{1,9},{9,17},{17,25},{26,2},{2,... | collective-permute-start | bytes 1572872 | tf_op jit(solution)/shard_map/while/body/eval_jaxpr/ppermute | solution.py:17
  758.7 9.6 %copy-start.3 = (bf16[4,16,1024]{2,1,0:T(8,128)(2,1)S(1)}, bf16[4,16,1024]{2,1,0:T(8,128)(2,1)}, u32[]{:S(2)}) copy-start(bf16[4,16,1024]{2,1,0:T(8,128)(2,1)} %get-tuple-element.385) | copy-start | bytes 393220 | tf_op jit(solution)/shard_map/while
  776.6 8.7 %collective-permute-start = (f32[16,8192]{1,0:T(8,128)S(1)}, f32[16,8192]{1,0:T(8,128)S(1)}, u32[]{:S(2)}, u32[]{:S(2)}) collective-permute-start(f32[16,8192]{1,0:T(8,128)S(1)} %bitcast_add_fusion.2), channel_id=1, source_target_pairs={{24,0},{0,8},{8,16},{16,24},{25,1},{1,9},{9,17},{17,25},{26,2},{2,... | collective-permute-start | bytes 1572872 | tf_op jit(solution)/shard_map/while/body/eval_jaxpr/ppermute | solution.py:17
  (83 other events, 162.8 us)
where the time goes:
time: 797 us; the launch traced here: 785 us
  local copies, waits for them, and re-layouts  271 us (34%)
  other arithmetic  222 us (28%)
  matrix products  174 us (22%)
  waiting for transfers between devices  69.2 us (9%)
  starting transfers between devices  45.8 us (6%)
    slice x16, local copies, waits for them, and re-layouts, attend(): prompt_vals = prompt[:, half:].reshape(-1, KV_HEADS, HEAD_DIM)  64.9 us
    reduce_sum x16, other arithmetic, attend(): jnp.sum(prompt_exp, -1, keepdims=True)  59.2 us
    ppermute x16, waiting for transfers between devices, passed_along(): return lax.ppermute(block, axis, route)  52 us
    dot_general x16, matrix products, attend(): jnp.einsum('pkgn,nkd->pkgd', (prompt_exp / denominator).astype(jnp.bfloat...  43.2 us
    dot_general x16, matrix products, attend(): jnp.einsum('pkgd,nkd->pkgn', queries, prompt_keys, preferred_element_type...  43.1 us
    ppermute x16, starting transfers between devices, passed_along(): return lax.ppermute(block, axis, route)  40.3 us
    while x304, local copies, waits for them, and re-layouts  35.5 us
    dot_general x16, matrix products, attend(): jnp.einsum('pkgd,pnkd->pkgn', queries, past_keys, preferred_element_type=...  34.2 us
  transfers between devices with their start and end apart: 17, of which 17 were waited for; matrix products, arithmetic and copies ran while one was open for 7% of the time, Pallas kernels for 0%

commit v1 on v0

v1 whole, which is shorter than its diff:
```python
import functools
import math
import jax
import jax.numpy as jnp
from jax import lax
from jax.experimental import pallas as pl
from jax.experimental.pallas import tpu as pltpu
from jax.sharding import PartitionSpec as P

HEADS = 64
KV_HEADS = 8
HEAD_DIM = 128
SHARE = HEADS // KV_HEADS
HALF = KV_HEADS * HEAD_DIM
GROUPS = 4
CHUNKS = 2
NEG_FILL = -1e30
MESH = pl.DeviceIdType.MESH
VMEM_LIMIT = 48 * 1024 * 1024


def round_kernel(
    sections,
    shards,
    steps,
    groups,
    hist,
    tok_ref,
    gain_ref,
    pkt_ref,
    prompt_ref,
    okt_ref,
    cache_ref,
    outgoing_ref,
    out_ref,
    incoming_ref,
    slots,
    sent,
    hidden,
    queries,
    pv_ref,
    ov_ref,
    send_sem,
    recv_sem,
    fork_send,
    fork_recv,
    own_sem,
    value_sem,
):
    half = pl.ds(HALF, HALF)
    prompt_values = pltpu.make_async_copy(prompt_ref.at[0, :, half], pv_ref, value_sem.at[0])
    own_values = pltpu.make_async_copy(cache_ref.at[:, :, half], ov_ref, value_sem.at[1])
    prompt_values.start()
    own_values.start()
    sec = lax.axis_index("section")
    me = lax.axis_index("dp")
    after = lax.rem(sec + 1, sections)
    before = lax.rem(sec + sections - 1, sections)
    items = steps * groups
    rows = slots.shape[2]
    width = rows // SHARE
    per = okt_ref.shape[2] // width
    model = HEADS * HEAD_DIM
    chunk_heads = KV_HEADS // CHUNKS

    barrier = pltpu.get_barrier_semaphore()
    pl.semaphore_signal(barrier, inc=1, device_id=(after, me), device_id_type=MESH)
    pl.semaphore_signal(barrier, inc=1, device_id=(before, me), device_id_type=MESH)

    def greet(off, carry):
        peer = lax.rem(me + off, shards)
        pl.semaphore_signal(barrier, inc=1, device_id=(sec, peer), device_id_type=MESH)
        return carry

    lax.fori_loop(1, shards, greet, 0)
    pl.semaphore_wait(barrier, 2 + shards - 1)

    def fork_copy(off):
        peer = lax.rem(me + off, shards)
        return pltpu.make_async_remote_copy(
            src_ref=outgoing_ref.at[peer],
            dst_ref=incoming_ref.at[me],
            send_sem=fork_send.at[off],
            recv_sem=fork_recv.at[off],
            device_id=(sec, peer),
            device_id_type=MESH,
        )

    def fork_start(off, carry):
        fork_copy(off).start()
        return carry

    lax.fori_loop(1, shards, fork_start, 0)
    own = pltpu.make_async_copy(outgoing_ref.at[me], incoming_ref.at[me], own_sem)
    own.start()

    last = sec == sections - 1

    def pass_copy(item, chunk):
        target = jnp.where(last, item + groups, item)
        target = lax.rem(target, items)
        heads = pl.ds(chunk * chunk_heads, chunk_heads)
        return pltpu.make_async_remote_copy(
            src_ref=sent.at[item, heads],
            dst_ref=slots.at[target, heads],
            send_sem=send_sem.at[item, chunk],
            recv_sem=recv_sem.at[target, chunk],
            device_id=(after, me),
            device_id_type=MESH,
        )

    def arrive(item):
        for chunk in range(CHUNKS):
            heads = pl.ds(chunk * chunk_heads, chunk_heads)
            pltpu.make_async_remote_copy(
                src_ref=sent.at[item, heads],
                dst_ref=slots.at[item, heads],
                send_sem=send_sem.at[item, chunk],
                recv_sem=recv_sem.at[item, chunk],
                device_id=(after, me),
                device_id_type=MESH,
            ).wait_recv()

    def inverse_norm(values):
        total = jnp.sum(values * values, axis=0).reshape(width, SHARE, HEAD_DIM)
        total = jnp.sum(jnp.sum(total, axis=2, keepdims=True), axis=1, keepdims=True)
        return lax.rsqrt(total * (1.0 / model) + 1e-05)

    def scaled(values, factor):
        shaped = values.reshape(KV_HEADS, width, SHARE, HEAD_DIM)
        return shaped * factor[None]

    factor = HEAD_DIM ** (-0.5) * math.log2(math.e)
    own_row = lax.broadcasted_iota(jnp.int32, (rows, width * per), 0) // SHARE
    own_col = lax.broadcasted_iota(jnp.int32, (rows, width * per), 1)
    same = own_row == own_col // per
    place = own_col % per

    def step(item, carry):
        now = item // groups
        group = lax.rem(item, groups)

        @pl.when((sec == 0) & (now == 0))
        def _():
            hidden[...] = tok_ref[item].astype(jnp.float32)

        @pl.when((sec == 0) & (now > 0))
        def _():
            arrive(item)
            got = slots[item]
            carried = scaled(got, inverse_norm(got)).reshape(got.shape)
            hidden[...] = tok_ref[item].astype(jnp.float32) + carried

        @pl.when(sec > 0)
        def _():
            arrive(item)
            hidden[...] = slots[item]

        held = hidden[...]
        normed = scaled(held, inverse_norm(held)) * gain_ref[...][:, None]
        queries[...] = normed.reshape(held.shape).astype(jnp.bfloat16)
        present = same & (place <= hist + now)

        for head in range(KV_HEADS):
            lanes = pl.ds(head * HEAD_DIM, HEAD_DIM)
            query = queries[head]
            shared = jnp.dot(query, pkt_ref[lanes, :], preferred_element_type=jnp.float32)
            alone = jnp.dot(
                query, okt_ref[group, lanes, :], preferred_element_type=jnp.float32
            )
            alone = jnp.where(present, alone, NEG_FILL)
            highest = jnp.maximum(
                jnp.max(shared, -1, keepdims=True), jnp.max(alone, -1, keepdims=True)
            )
            shared = jnp.exp2((shared - highest) * factor)
            alone = jnp.exp2((alone - highest) * factor)
            total = jnp.sum(shared, -1, keepdims=True) + jnp.sum(alone, -1, keepdims=True)
            inverse = 1.0 / total
            mixed = jnp.dot(
                (shared * inverse).astype(jnp.bfloat16),
                pv_ref[:, lanes],
                preferred_element_type=jnp.float32,
            )
            mixed = mixed + jnp.dot(
                (alone * inverse).astype(jnp.bfloat16),
                ov_ref[group, :, lanes],
                preferred_element_type=jnp.float32,
            )
            out_ref[item, head] = mixed.astype(jnp.bfloat16)
            sent[item, head] = hidden[head] + mixed
            if head % chunk_heads == chunk_heads - 1:

                @pl.when(jnp.logical_not(last) | (now < steps - 1))
                def _():
                    pass_copy(item, head // chunk_heads).start()

        return carry

    prompt_values.wait()
    own_values.wait()
    lax.fori_loop(0, items, step, 0)

    def sent_done(item, carry):
        @pl.when(jnp.logical_not(last) | (item < items - groups))
        def _():
            for chunk in range(CHUNKS):
                pass_copy(item, chunk).wait_send()

        return carry

    lax.fori_loop(0, items, sent_done, 0)

    def fork_done(off, carry):
        fork_copy(off).wait()
        return carry

    lax.fori_loop(1, shards, fork_done, 0)
    own.wait()


def pick_kernel(count, index_ref, src_ref, dst_ref, sems):
    def begin(i, carry):
        pltpu.make_async_copy(src_ref.at[index_ref[i]], dst_ref.at[i], sems.at[i]).start()
        return carry

    def finish(i, carry):
        pltpu.make_async_copy(src_ref.at[index_ref[i]], dst_ref.at[i], sems.at[i]).wait()
        return carry

    lax.fori_loop(0, count, begin, 0)
    lax.fori_loop(0, count, finish, 0)


def pick(source, index):
    count = index.shape[0]
    return pl.pallas_call(
        functools.partial(pick_kernel, count),
        out_shape=jax.ShapeDtypeStruct((count,) + source.shape[1:], source.dtype),
        in_specs=[
            pl.BlockSpec(memory_space=pltpu.SMEM),
            pl.BlockSpec(memory_space=pl.ANY),
        ],
        out_specs=pl.BlockSpec(memory_space=pl.ANY),
        scratch_shapes=[pltpu.SemaphoreType.DMA((count,))],
    )(index, source)


def local(token_states, norm_gains, prompt_kv, history_kv, new_kv, ancestors):
    sections = lax.axis_size("section")
    shards = lax.axis_size("dp")
    own_index = lax.axis_index("dp")
    part_dev, hist = history_kv.shape[1:3]
    steps = new_kv.shape[1]
    model = token_states.shape[2]
    per = hist + steps
    groups = GROUPS
    width = part_dev // groups
    rows = width * SHARE
    items = steps * groups

    cache = jnp.concatenate([history_kv[0], jnp.transpose(new_kv[0], (1, 0, 2))], axis=1)
    owners = ancestors.reshape(shards, part_dev)
    picked = jnp.max(
        jnp.where(owners // part_dev == own_index, owners % part_dev, 0), axis=1
    )
    outgoing = pick(cache, picked)

    tokens = token_states.reshape(steps, groups, width, KV_HEADS, SHARE, HEAD_DIM)
    tokens = jnp.transpose(tokens, (0, 1, 3, 2, 4, 5)).reshape(items, KV_HEADS, rows, HEAD_DIM)
    gains = norm_gains.reshape(KV_HEADS, SHARE, HEAD_DIM)
    prompt_keys = jnp.transpose(prompt_kv[0, :, :HALF])
    grouped = cache.reshape(groups, width * per, 2 * HALF)
    own_keys = jnp.transpose(grouped[:, :, :HALF], (0, 2, 1))

    whole = pl.BlockSpec(memory_space=pltpu.VMEM)
    prompt_len = prompt_kv.shape[1]
    mixed, incoming = pl.pallas_call(
        functools.partial(round_kernel, sections, shards, steps, groups, hist),
        out_shape=(
            jax.ShapeDtypeStruct((items, KV_HEADS, rows, HEAD_DIM), jnp.bfloat16),
            jax.ShapeDtypeStruct((shards, per, 2 * HALF), jnp.bfloat16),
        ),
        in_specs=[
            whole,
            whole,
            whole,
            pl.BlockSpec(memory_space=pl.ANY),
            whole,
            pl.BlockSpec(memory_space=pl.ANY),
            pl.BlockSpec(memory_space=pl.ANY),
        ],
        out_specs=(whole, pl.BlockSpec(memory_space=pl.ANY)),
        scratch_shapes=[
            pltpu.VMEM((items, KV_HEADS, rows, HEAD_DIM), jnp.float32),
            pltpu.VMEM((items, KV_HEADS, rows, HEAD_DIM), jnp.float32),
            pltpu.VMEM((KV_HEADS, rows, HEAD_DIM), jnp.float32),
            pltpu.VMEM((KV_HEADS, rows, HEAD_DIM), jnp.bfloat16),
            pltpu.VMEM((prompt_len, HALF), jnp.bfloat16),
            pltpu.VMEM((groups, width * per, HALF), jnp.bfloat16),
            pltpu.SemaphoreType.DMA((items, CHUNKS)),
            pltpu.SemaphoreType.DMA((items, CHUNKS)),
            pltpu.SemaphoreType.DMA((shards,)),
            pltpu.SemaphoreType.DMA((shards,)),
            pltpu.SemaphoreType.DMA,
            pltpu.SemaphoreType.DMA((2,)),
        ],
        compiler_params=pltpu.CompilerParams(
            collective_id=0, has_side_effects=True, vmem_limit_bytes=VMEM_LIMIT
        ),
    )(tokens, gains, prompt_keys, prompt_kv, own_keys, grouped, outgoing)

    mixed = mixed.reshape(steps, groups, KV_HEADS, width, SHARE, HEAD_DIM)
    mixed = jnp.transpose(mixed, (0, 1, 3, 2, 4, 5)).reshape(1, steps, part_dev, model)
    own_ancestors = lax.dynamic_slice_in_dim(ancestors, own_index * part_dev, part_dev)
    forked = pick(incoming, own_ancestors // part_dev)
    return (mixed, forked[None])


def solution(mesh):
    in_specs = (
        P(None, "dp", None),
        P("section", None),
        P("section", None, None),
        P("section", "dp", None, None),
        P("section", None, "dp", None),
        P(),
    )
    out_specs = (P("section", None, "dp", None), P("section", "dp", None, None))
    return jax.shard_map(local, mesh=mesh, in_specs=in_specs, out_specs=out_specs, check_vma=False)
```

time: 797 us -> 222 us (0.28); the launches traced: 785 us -> 221 us
  local copies, waits for them, and re-layouts: 271 us -> 17 us
  other arithmetic: 222 us -> 3.59 us
  Pallas kernels: 0 us -> 200 us
  matrix products: 174 us -> 0 us
  waiting for transfers between devices: 69.2 us -> 0 us
  starting transfers between devices: 45.8 us -> 0 us
    pallas_call x0 -> x3, Pallas kernels: none -> 200 us  [the longest x1 101 us: local(): pl.pallas_call(functools.partial(round_kernel, sections, shards, steps, g...]
    dot_general x96 -> x0, matrix products: 174 us -> none  [the longest x16 43.2 us: attend(): jnp.einsum('pkgn,nkd->pkgd', (prompt_exp / denominator).astype(jnp.bfloat...]
    reduce_sum x80 -> x0, other arithmetic: 124 us -> none  [the longest x16 59.2 us: attend(): jnp.sum(prompt_exp, -1, keepdims=True)]
    slice x48 -> x1, local copies, waits for them, and re-layouts: 93.3 us -> 3.08 us  [local(): prompt_keys = jnp.transpose(prompt_kv[0, :, :HALF])]
    ppermute x16 -> x0, waiting for transfers between devices: 52 us -> none  [passed_along(): return lax.ppermute(block, axis, route)]
    reduce_sum x48 -> x0, local copies, waits for them, and re-layouts: 46.3 us -> none  [the longest x16 24.3 us: attend(): jnp.sum(prompt_exp, -1, keepdims=True)]
    ppermute x16 -> x0, starting transfers between devices: 40.3 us -> none  [passed_along(): return lax.ppermute(block, axis, route)]
    reduce_max x48 -> x0, local copies, waits for them, and re-layouts: 36.6 us -> none  [the longest x16 14.7 us: attend(): jnp.max(past_scores, -1, keepdims=True)]
  transfers between devices with their start and end apart: 17 -> 0, of which waited for: 17 -> 0; matrix products, arithmetic and copies ran while one was open for 7% -> 0% of each run, Pallas kernels for 0% -> 0%
where the time goes in v1:
time: 222 us; the launch traced here: 221 us
  Pallas kernels  200 us (90%)
  local copies, waits for them, and re-layouts  17 us (8%)
  other arithmetic  3.59 us (2%)
    pallas_call x1, Pallas kernels, local(): pl.pallas_call(functools.partial(round_kernel, sections, shards, steps, g...  101 us
    pallas_call x2, Pallas kernels, pick(): pl.pallas_call(functools.partial(pick_kernel, count), out_shape=jax.Shape...  99.2 us
    unnamed x14, local copies, waits for them, and re-layouts  8.8 us

profile of v1, /device:TPU:5, one launch (start us, length us, event | category | flops | bytes accessed | tf_op | source)
XLA Modules:
  0.0 221.4 jit_solution(2277073582396539655)
XLA Ops:
  0.6 1.3 and_select_fusion.index_ref
  1.9 0.7 reshape.29
  2.6 0.6 fusion.2.index_ref
  3.3 1.2 copy.19
  4.4 0.0 copy-start.4
  4.5 1.6 copy.15
  6.1 0.2 copy.8
  6.3 0.0 copy-done.4
  6.3 1.0 copy.18
  7.3 1.7 pad_maximum_fusion.src_ref
  9.0 0.0 copy-start.3
  9.0 33.7 %shard_map.77.outgoing_ref = bf16[8,32,2048]{2,1,0:T(8,128)(2,1)} custom-call(s32[8]{0:T(128)} %fusion.2.index_ref, bf16[16,32,2048]{2,1,0:T(8,128)(2,1)} %pad_maximum_fusion.src_ref), custom_call_target="tpu_custom_call" | custom-call | tf_op jit(solution)/shard_map/pallas_call | solution.py:236
  42.8 0.0 copy-done.3
  42.8 1.1 slice_bitcast_fusion
  43.8 1.6 copy.12.okt_ref
  45.4 3.1 %slice.6 = bf16[1,1024,1024]{2,1,0:T(8,128)(2,1)} slice(bf16[1,1024,2048]{2,1,0:T(8,128)(2,1)} %prompt_ref.1), slice={[0:1], [0:1024], [0:1024]} | slice | bytes 4194304 | tf_op jit(solution)/shard_map/slice | solution.py:271
  48.5 0.0 copy-start
  48.5 0.0 copy-start.2
  48.5 4.0 %copy.14 = bf16[1,1024,1024]{1,2,0:T(8,128)(2,1)} copy(bf16[1,1024,1024]{2,1,0:T(8,128)(2,1)} %slice.6) | data formatting | bytes 4194304
  52.5 0.0 copy-done
  52.5 0.0 copy-done.2
  52.6 100.9 %shard_map.78 = (bf16[16,8,32,128]{3,2,1,0:T(8,128)(2,1)S(1)}, bf16[8,32,2048]{2,1,0:T(8,128)(2,1)S(1)}) custom-call(bf16[16,8,32,128]{3,2,1,0:T(8,128)(2,1)S(1)} %bitcast.28, f32[8,8,128]{2,1,0:T(8,128)S(1)} %bitcast.30, bf16[1024,1024]{1,0:T(8,128)(2,1)} %bitcast.34, bf16[1,1024,2048]{2,1,0:T(8,128)(2,1)} %prompt_ref.1, ...), custom_call_target="tpu_custom_call" | custom-call | tf_op jit(solution)/shard_map/pallas_call | solution.py:277
  153.5 0.0 copy-start.1
  153.5 1.0 copy-done.1
  154.5 0.3 copy.13
  154.7 1.3 reshape.31
  156.0 65.4 %shard_map.79 = bf16[16,32,2048]{2,1,0:T(8,128)(2,1)} custom-call(s32[16]{0:T(128)} %and_select_fusion.index_ref, bf16[8,32,2048]{2,1,0:T(8,128)(2,1)} %copy-done.1), custom_call_target="tpu_custom_call" | custom-call | tf_op jit(solution)/shard_map/pallas_call | solution.py:236
Async XLA Ops:
  4.4 1.9 copy-start.4
  9.0 33.7 %copy-start.3 = (bf16[16,32,2048]{2,1,0:T(8,128)(2,1)S(1)}, bf16[16,32,2048]{2,1,0:T(8,128)(2,1)}, u32[]{:S(2)}) copy-start(bf16[16,32,2048]{2,1,0:T(8,128)(2,1)} %pad_maximum_fusion.src_ref) | copy-start | bytes 6291460
  48.5 4.0 %copy-start = (bf16[8,32,2048]{2,1,0:T(8,128)(2,1)S(1)}, bf16[8,32,2048]{2,1,0:T(8,128)(2,1)}, u32[]{:S(2)}) copy-start(bf16[8,32,2048]{2,1,0:T(8,128)(2,1)} %shard_map.77.outgoing_ref) | copy-start | bytes 3145732
  48.5 4.0 %copy-start.2 = (f32[1,8192]{1,0:T(1,128)S(1)}, f32[1,8192]{1,0:T(1,128)}, u32[]{:S(2)}) copy-start(f32[1,8192]{1,0:T(1,128)} %param.7) | copy-start | bytes 98308
  153.5 1.0 copy-start.1

commit v2 on v1

--- a/solution.py
+++ b/solution.py
@@ -16,7 +16,7 @@
 CHUNKS = 2
 NEG_FILL = -1e30
 MESH = pl.DeviceIdType.MESH
-VMEM_LIMIT = 48 * 1024 * 1024
+VMEM_LIMIT = 56 * 1024 * 1024
 
 
 def round_kernel(
@@ -27,29 +27,32 @@
     hist,
     tok_ref,
     gain_ref,
-    pkt_ref,
     prompt_ref,
-    okt_ref,
     cache_ref,
-    outgoing_ref,
+    picked_ref,
+    source_ref,
     out_ref,
-    incoming_ref,
+    forked_ref,
     slots,
     sent,
     hidden,
     queries,
     pv_ref,
     ov_ref,
+    pkt_ref,
+    okt_ref,
+    scores,
+    weights,
+    outgoing,
+    incoming,
     send_sem,
     recv_sem,
     fork_send,
     fork_recv,
-    own_sem,
     value_sem,
 ):
-    half = pl.ds(HALF, HALF)
-    prompt_values = pltpu.make_async_copy(prompt_ref.at[0, :, half], pv_ref, value_sem.at[0])
-    own_values = pltpu.make_async_copy(cache_ref.at[:, :, half], ov_ref, value_sem.at[1])
+    prompt_values = pltpu.make_async_copy(prompt_ref.at[0], pv_ref, value_sem.at[0])
+    own_values = pltpu.make_async_copy(cache_ref, ov_ref, value_sem.at[1])
     prompt_values.start()
     own_values.start()
     sec = lax.axis_index("section")
@@ -59,8 +62,10 @@
     items = steps * groups
     rows = slots.shape[2]
     width = rows // SHARE
-    per = okt_ref.shape[2] // width
+    per = cache_ref.shape[1]
     model = HEADS * HEAD_DIM
+    prompt_len = pv_ref.shape[0]
+    part_dev = forked_ref.shape[0]
     chunk_heads = KV_HEADS // CHUNKS
 
     barrier = pltpu.get_barrier_semaphore()
@@ -78,21 +83,27 @@
     def fork_copy(off):
         peer = lax.rem(me + off, shards)
         return pltpu.make_async_remote_copy(
-            src_ref=outgoing_ref.at[peer],
-            dst_ref=incoming_ref.at[me],
+            src_ref=outgoing.at[off],
+            dst_ref=incoming.at[me],
             send_sem=fork_send.at[off],
             recv_sem=fork_recv.at[off],
             device_id=(sec, peer),
             device_id_type=MESH,
         )
 
+    prompt_values.wait()
+    own_values.wait()
+
+    def from_cache(index):
+        return ov_ref[index]
+
     def fork_start(off, carry):
+        outgoing[off] = from_cache(picked_ref[lax.rem(me + off, shards)])
         fork_copy(off).start()
         return carry
 
     lax.fori_loop(1, shards, fork_start, 0)
-    own = pltpu.make_async_copy(outgoing_ref.at[me], incoming_ref.at[me], own_sem)
-    own.start()
+    incoming[me] = from_cache(picked_ref[me])
 
     last = sec == sections - 1
 
@@ -139,6 +150,7 @@
     def step(item, carry):
         now = item // groups
         group = lax.rem(item, groups)
+        members = pl.ds(group * width, width)
 
         @pl.when((sec == 0) & (now == 0))
         def _():
@@ -164,26 +176,31 @@
         for head in range(KV_HEADS):
             lanes = pl.ds(head * HEAD_DIM, HEAD_DIM)
             query = queries[head]
-            shared = jnp.dot(query, pkt_ref[lanes, :], preferred_element_type=jnp.float32)
+            scores[head, :, :prompt_len] = jnp.dot(
+                query, pkt_ref[lanes, :], preferred_element_type=jnp.float32
+            )
             alone = jnp.dot(
                 query, okt_ref[group, lanes, :], preferred_element_type=jnp.float32
             )
-            alone = jnp.where(present, alone, NEG_FILL)
-            highest = jnp.maximum(
-                jnp.max(shared, -1, keepdims=True), jnp.max(alone, -1, keepdims=True)
-            )
-            shared = jnp.exp2((shared - highest) * factor)
-            alone = jnp.exp2((alone - highest) * factor)
-            total = jnp.sum(shared, -1, keepdims=True) + jnp.sum(alone, -1, keepdims=True)
-            inverse = 1.0 / total
+            scores[head, :, prompt_len:] = jnp.where(present, alone, NEG_FILL)
+
+        for head in range(KV_HEADS):
+            raw = scores[head]
+            highest = jnp.max(raw, -1, keepdims=True)
+            raised = jnp.exp2((raw - highest) * factor)
+            inverse = 1.0 / jnp.sum(raised, -1, keepdims=True)
+            weights[head] = (raised * inverse).astype(jnp.bfloat16)
+
+        for head in range(KV_HEADS):
+            lanes = pl.ds(HALF + head * HEAD_DIM, HEAD_DIM)
             mixed = jnp.dot(
-                (shared * inverse).astype(jnp.bfloat16),
+                weights[head, :, :prompt_len],
                 pv_ref[:, lanes],
                 preferred_element_type=jnp.float32,
             )
             mixed = mixed + jnp.dot(
-                (alone * inverse).astype(jnp.bfloat16),
-                ov_ref[group, :, lanes],
+                weights[head, :, prompt_len:],
+                ov_ref[members, :, lanes].reshape(width * per, HEAD_DIM),
                 preferred_element_type=jnp.float32,
             )
             out_ref[item, head] = mixed.astype(jnp.bfloat16)
@@ -196,8 +213,12 @@
 
         return carry
 
-    prompt_values.wait()
-    own_values.wait()
+    for head in range(KV_HEADS):
+        lanes = pl.ds(head * HEAD_DIM, HEAD_DIM)
+        pkt_ref[lanes, :] = pv_ref[:, lanes].T
+        for group in range(groups):
+            block = ov_ref[pl.ds(group * width, width), :, lanes]
+            okt_ref[group, lanes, :] = block.reshape(width * per, HEAD_DIM).T
     lax.fori_loop(0, items, step, 0)
 
     def sent_done(item, carry):
@@ -215,34 +236,12 @@
         return carry
 
     lax.fori_loop(1, shards, fork_done, 0)
-    own.wait()
-
-
-def pick_kernel(count, index_ref, src_ref, dst_ref, sems):
-    def begin(i, carry):
-        pltpu.make_async_copy(src_ref.at[index_ref[i]], dst_ref.at[i], sems.at[i]).start()
-        return carry
-
-    def finish(i, carry):
-        pltpu.make_async_copy(src_ref.at[index_ref[i]], dst_ref.at[i], sems.at[i]).wait()
-        return carry
-
-    lax.fori_loop(0, count, begin, 0)
-    lax.fori_loop(0, count, finish, 0)
-
-
-def pick(source, index):
-    count = index.shape[0]
-    return pl.pallas_call(
-        functools.partial(pick_kernel, count),
-        out_shape=jax.ShapeDtypeStruct((count,) + source.shape[1:], source.dtype),
-        in_specs=[
-            pl.BlockSpec(memory_space=pltpu.SMEM),
-            pl.BlockSpec(memory_space=pl.ANY),
-        ],
-        out_specs=pl.BlockSpec(memory_space=pl.ANY),
-        scratch_shapes=[pltpu.SemaphoreType.DMA((count,))],
-    )(index, source)
+
+    def fork_place(i, carry):
+        forked_ref[i] = incoming[source_ref[i]]
+        return carry
+
+    lax.fori_loop(0, part_dev, fork_place, 0)
 
 
 def local(token_states, norm_gains, prompt_kv, history_kv, new_kv, ancestors):
@@ -263,56 +262,56 @@
     picked = jnp.max(
         jnp.where(owners // part_dev == own_index, owners % part_dev, 0), axis=1
     )
-    outgoing = pick(cache, picked)
+    own_ancestors = lax.dynamic_slice_in_dim(ancestors, own_index * part_dev, part_dev)
+    sources = own_ancestors // part_dev
 
     tokens = token_states.reshape(steps, groups, width, KV_HEADS, SHARE, HEAD_DIM)
     tokens = jnp.transpose(tokens, (0, 1, 3, 2, 4, 5)).reshape(items, KV_HEADS, rows, HEAD_DIM)
     gains = norm_gains.reshape(KV_HEADS, SHARE, HEAD_DIM)
-    prompt_keys = jnp.transpose(prompt_kv[0, :, :HALF])
-    grouped = cache.reshape(groups, width * per, 2 * HALF)
-    own_keys = jnp.transpose(grouped[:, :, :HALF], (0, 2, 1))
 
     whole = pl.BlockSpec(memory_space=pltpu.VMEM)
     prompt_len = prompt_kv.shape[1]
-    mixed, incoming = pl.pallas_call(
+    mixed, forked = pl.pallas_call(
         functools.partial(round_kernel, sections, shards, steps, groups, hist),
         out_shape=(
             jax.ShapeDtypeStruct((items, KV_HEADS, rows, HEAD_DIM), jnp.bfloat16),
-            jax.ShapeDtypeStruct((shards, per, 2 * HALF), jnp.bfloat16),
+            jax.ShapeDtypeStruct((part_dev, per, 2 * HALF), jnp.bfloat16),
         ),
         in_specs=[
             whole,
             whole,
-            whole,
-            pl.BlockSpec(memory_space=pl.ANY),
-            whole,
             pl.BlockSpec(memory_space=pl.ANY),
             pl.BlockSpec(memory_space=pl.ANY),
+            pl.BlockSpec(memory_space=pltpu.SMEM),
+            pl.BlockSpec(memory_space=pltpu.SMEM),
         ],
-        out_specs=(whole, pl.BlockSpec(memory_space=pl.ANY)),
+        out_specs=(whole, whole),
         scratch_shapes=[
             pltpu.VMEM((items, KV_HEADS, rows, HEAD_DIM), jnp.float32),
             pltpu.VMEM((items, KV_HEADS, rows, HEAD_DIM), jnp.float32),
             pltpu.VMEM((KV_HEADS, rows, HEAD_DIM), jnp.float32),
             pltpu.VMEM((KV_HEADS, rows, HEAD_DIM), jnp.bfloat16),
-            pltpu.VMEM((prompt_len, HALF), jnp.bfloat16),
-            pltpu.VMEM((groups, width * per, HALF), jnp.bfloat16),
+            pltpu.VMEM((prompt_len, 2 * HALF), jnp.bfloat16),
+            pltpu.VMEM((part_dev, per, 2 * HALF), jnp.bfloat16),
+            pltpu.VMEM((HALF, prompt_len), jnp.bfloat16),
+            pltpu.VMEM((groups, HALF, width * per), jnp.bfloat16),
+            pltpu.VMEM((KV_HEADS, rows, prompt_len + width * per), jnp.float32),
+            pltpu.VMEM((KV_HEADS, rows, prompt_len + width * per), jnp.bfloat16),
+            pltpu.VMEM((shards, per, 2 * HALF), jnp.bfloat16),
+            pltpu.VMEM((shards, per, 2 * HALF), jnp.bfloat16),
             pltpu.SemaphoreType.DMA((items, CHUNKS)),
             pltpu.SemaphoreType.DMA((items, CHUNKS)),
             pltpu.SemaphoreType.DMA((shards,)),
             pltpu.SemaphoreType.DMA((shards,)),
-            pltpu.SemaphoreType.DMA,
             pltpu.SemaphoreType.DMA((2,)),
         ],
         compiler_params=pltpu.CompilerParams(
             collective_id=0, has_side_effects=True, vmem_limit_bytes=VMEM_LIMIT
         ),
-    )(tokens, gains, prompt_keys, prompt_kv, own_keys, grouped, outgoing)
+    )(tokens, gains, prompt_kv, cache, picked, sources)
 
     mixed = mixed.reshape(steps, groups, KV_HEADS, width, SHARE, HEAD_DIM)
     mixed = jnp.transpose(mixed, (0, 1, 3, 2, 4, 5)).reshape(1, steps, part_dev, model)
-    own_ancestors = lax.dynamic_slice_in_dim(ancestors, own_index * part_dev, part_dev)
-    forked = pick(incoming, own_ancestors // part_dev)
     return (mixed, forked[None])
 
 

time: 222 us -> 80.2 us (0.36)
  Pallas kernels: 200 us -> 65.7 us
  local copies, waits for them, and re-layouts: 17 us -> 9.95 us
    pallas_call x2 -> x0, Pallas kernels: 99.2 us -> none  [pick(): pl.pallas_call(functools.partial(pick_kernel, count), out_shape=jax.Shape...]
    pallas_call x1, Pallas kernels: 101 us -> 65.7 us  [local(): pl.pallas_call(functools.partial(round_kernel, sections, shards, steps, g...]
    unnamed x14 -> x8, local copies, waits for them, and re-layouts: 8.8 us -> 5.14 us
    slice x1 -> x0, local copies, waits for them, and re-layouts: 3.08 us -> none  [local(): prompt_keys = jnp.transpose(prompt_kv[0, :, :HALF])]
    transpose x2 -> x0, local copies, waits for them, and re-layouts: 2.67 us -> none  [local(): own_keys = jnp.transpose(grouped[:, :, :HALF], (0, 2, 1))]
where the time goes in v2:
time: 80.2 us; the launch traced here: 80 us
  Pallas kernels  65.7 us (82%)
  local copies, waits for them, and re-layouts  9.95 us (12%)
  other arithmetic  3.64 us (5%)
    pallas_call x1, Pallas kernels, local(): pl.pallas_call(functools.partial(round_kernel, sections, shards, steps, g...  65.7 us
    unnamed x8, local copies, waits for them, and re-layouts  5.14 us
    concatenate x1, other arithmetic, local(): jnp.concatenate([history_kv[0], jnp.transpose(new_kv[0], (1, 0, 2))], axi...  1.66 us
    transpose x1, local copies, waits for them, and re-layouts, local(): jnp.transpose(mixed, (0, 1, 3, 2, 4, 5)).reshape(1, steps, part_dev, model)  1.64 us

profile of v2, /device:TPU:5, one launch (start us, length us, event | category | flops | bytes accessed | tf_op | source)
XLA Modules:
  0.0 80.0 jit_solution(17467442469033986788)
XLA Ops:
  0.6 1.3 %and_select_fusion.source_ref = s32[16]{0:T(128)} fusion(s32[128]{0:T(128)} %param.11, s32[]{:T(128)S(6)} %select_n.27), kind=kLoop, calls=%fused_computation.14 | loop fusion | flops 240 | bytes 132 | tf_op jit(solution)/shard_map/jit(floor_divide)/jit(_where)/select_n | solution.py:266
  2.0 0.7 reshape.25
  2.7 0.7 fusion.2.picked_ref
  3.3 1.2 %copy.16 = bf16[1,4,16,2048]{3,1,2,0:T(4,128)(2,1)S(1)} copy(bf16[1,4,16,2048]{3,2,1,0:T(8,128)(2,1)} %param.10) | data formatting | bytes 524288 | tf_op args[4]
  4.5 0.0 copy-start.1
  4.5 1.6 %copy.12 = bf16[8,8,64,128]{3,2,1,0:T(8,128)(2,1)S(1)} copy(bf16[8,8,64,128]{3,1,2,0:T(8,128)(2,1)} %bitcast.27) | data formatting | bytes 2097152
  6.2 1.2 %copy.8 = bf16[4,4,4,8,8,128]{5,4,2,3,1,0:T(8,128)(2,1)} copy(bf16[4,4,4,8,8,128]{5,4,3,2,1,0:T(8,128)(2,1)S(1)} %bitcast.23) | data formatting | bytes 2097152 | tf_op jit(solution)/shard_map/reshape | solution.py:268
  7.3 0.0 copy-done.1
  7.3 1.0 %copy.15 = bf16[1,16,28,2048]{3,2,1,0:T(8,128)(2,1)S(1)} copy(bf16[1,16,28,2048]{3,1,2,0:T(8,128)(2,1)S(1)} %copy-done.1) | data formatting | bytes 3670016 | tf_op args[3]
  8.4 1.7 %pad_maximum_fusion.cache_ref = bf16[16,32,2048]{2,1,0:T(8,128)(2,1)} fusion(bf16[16,4,2048]{2,1,0:T(4,128)(2,1)S(1)} %bitcast.26, bf16[16,28,2048]{2,1,0:T(8,128)(2,1)S(1)} %bitcast.22), kind=kLoop, calls=%fused_computation | loop fusion | flops 4194304 | bytes 4194304 | tf_op jit(solution)/shard_map/concatenate | solution.py:260
  10.0 65.7 %shard_map.77 = (bf16[16,8,32,128]{3,2,1,0:T(8,128)(2,1)}, bf16[16,32,2048]{2,1,0:T(8,128)(2,1)}) custom-call(bf16[16,8,32,128]{3,2,1,0:T(8,128)(2,1)} %bitcast.24, f32[8,8,128]{2,1,0:T(8,128)} %bitcast.29, bf16[1,1024,2048]{2,1,0:T(8,128)(2,1)} %prompt_ref.1, bf16[16,32,2048]{2,1,0:T(8,128)(2,1)} %pad_maximum_fusion.cache_ref, s32[8]{0:T(128)} %fusion.2.picked_ref, ...), custom_call_target="tpu_custom_call" | custom-call | tf_op jit(solution)/shard_map/pallas_call | solution.py:274
  75.8 0.0 copy-start
  75.8 1.6 %copy.11 = bf16[4,4,4,8,8,128]{5,4,3,2,1,0:T(8,128)(2,1)S(1)} copy(bf16[4,4,4,8,8,128]{5,4,2,3,1,0:T(8,128)(2,1)} %bitcast.28) | data formatting | bytes 2097152 | tf_op jit(solution)/shard_map/transpose | solution.py:314
  77.4 1.3 %reshape.27 = bf16[1,4,16,8192]{3,2,1,0:T(8,128)(2,1)} reshape(bf16[4,4,4,8,8,128]{5,4,3,2,1,0:T(8,128)(2,1)S(1)} %copy.11) | data formatting | bytes 2097152 | tf_op jit(solution)/shard_map/reshape | solution.py:314
  78.7 0.0 copy-done
  78.7 1.3 %copy.18 = bf16[1,16,32,2048]{3,2,1,0:T(8,128)(2,1)} copy(bf16[1,16,32,2048]{3,2,1,0:T(8,128)(2,1)S(1)} %bitcast.25) | data formatting | bytes 4194304
Async XLA Ops:
  4.5 2.8 %copy-start.1 = (bf16[1,16,28,2048]{3,1,2,0:T(8,128)(2,1)S(1)}, bf16[1,16,28,2048]{3,1,2,0:T(8,128)(2,1)}, u32[]{:S(2)}) copy-start(bf16[1,16,28,2048]{3,1,2,0:T(8,128)(2,1)} %param.9) | copy-start | bytes 5505028
  75.8 2.9 %copy-start = (bf16[16,32,2048]{2,1,0:T(8,128)(2,1)S(1)}, bf16[16,32,2048]{2,1,0:T(8,128)(2,1)}, u32[]{:S(2)}) copy-start(bf16[16,32,2048]{2,1,0:T(8,128)(2,1)} %get-tuple-element.5) | copy-start | bytes 6291460

commit v3 on v2

--- a/solution.py
+++ b/solution.py
@@ -12,7 +12,7 @@
 HEAD_DIM = 128
 SHARE = HEADS // KV_HEADS
 HALF = KV_HEADS * HEAD_DIM
-GROUPS = 4
+GROUPS = 8
 CHUNKS = 2
 NEG_FILL = -1e30
 MESH = pl.DeviceIdType.MESH
@@ -43,6 +43,7 @@
     okt_ref,
     scores,
     weights,
+    mixes,
     outgoing,
     incoming,
     send_sem,
@@ -141,6 +142,12 @@
         shaped = values.reshape(KV_HEADS, width, SHARE, HEAD_DIM)
         return shaped * factor[None]
 
+    def embedded(item):
+        loaded = tok_ref[item].astype(jnp.float32)
+        loaded = loaded.reshape(width, KV_HEADS, SHARE, HEAD_DIM)
+        parts = [loaded[:, head].reshape(rows, HEAD_DIM) for head in range(KV_HEADS)]
+        return jnp.stack(parts, axis=0)
+
     factor = HEAD_DIM ** (-0.5) * math.log2(math.e)
     own_row = lax.broadcasted_iota(jnp.int32, (rows, width * per), 0) // SHARE
     own_col = lax.broadcasted_iota(jnp.int32, (rows, width * per), 1)
@@ -154,14 +161,14 @@
 
         @pl.when((sec == 0) & (now == 0))
         def _():
-            hidden[...] = tok_ref[item].astype(jnp.float32)
+            hidden[...] = embedded(item)
 
         @pl.when((sec == 0) & (now > 0))
         def _():
             arrive(item)
             got = slots[item]
             carried = scaled(got, inverse_norm(got)).reshape(got.shape)
-            hidden[...] = tok_ref[item].astype(jnp.float32) + carried
+            hidden[...] = embedded(item) + carried
 
         @pl.when(sec > 0)
         def _():
@@ -203,7 +210,7 @@
                 ov_ref[members, :, lanes].reshape(width * per, HEAD_DIM),
                 preferred_element_type=jnp.float32,
             )
-            out_ref[item, head] = mixed.astype(jnp.bfloat16)
+            mixes[:, pl.ds(head * SHARE, SHARE), :] = mixed.reshape(width, SHARE, HEAD_DIM)
             sent[item, head] = hidden[head] + mixed
             if head % chunk_heads == chunk_heads - 1:
 
@@ -211,6 +218,7 @@
                 def _():
                     pass_copy(item, head // chunk_heads).start()
 
+        out_ref[item] = mixes[...].astype(jnp.bfloat16)
         return carry
 
     for head in range(KV_HEADS):
@@ -265,8 +273,7 @@
     own_ancestors = lax.dynamic_slice_in_dim(ancestors, own_index * part_dev, part_dev)
     sources = own_ancestors // part_dev
 
-    tokens = token_states.reshape(steps, groups, width, KV_HEADS, SHARE, HEAD_DIM)
-    tokens = jnp.transpose(tokens, (0, 1, 3, 2, 4, 5)).reshape(items, KV_HEADS, rows, HEAD_DIM)
+    tokens = token_states.reshape(items, width, HEADS, HEAD_DIM)
     gains = norm_gains.reshape(KV_HEADS, SHARE, HEAD_DIM)
 
     whole = pl.BlockSpec(memory_space=pltpu.VMEM)
@@ -274,7 +281,7 @@
     mixed, forked = pl.pallas_call(
         functools.partial(round_kernel, sections, shards, steps, groups, hist),
         out_shape=(
-            jax.ShapeDtypeStruct((items, KV_HEADS, rows, HEAD_DIM), jnp.bfloat16),
+            jax.ShapeDtypeStruct((items, width, HEADS, HEAD_DIM), jnp.bfloat16),
             jax.ShapeDtypeStruct((part_dev, per, 2 * HALF), jnp.bfloat16),
         ),
         in_specs=[
@@ -297,6 +304,7 @@
             pltpu.VMEM((groups, HALF, width * per), jnp.bfloat16),
             pltpu.VMEM((KV_HEADS, rows, prompt_len + width * per), jnp.float32),
             pltpu.VMEM((KV_HEADS, rows, prompt_len + width * per), jnp.bfloat16),
+            pltpu.VMEM((width, HEADS, HEAD_DIM), jnp.float32),
             pltpu.VMEM((shards, per, 2 * HALF), jnp.bfloat16),
             pltpu.VMEM((shards, per, 2 * HALF), jnp.bfloat16),
             pltpu.SemaphoreType.DMA((items, CHUNKS)),
@@ -310,8 +318,7 @@
         ),
     )(tokens, gains, prompt_kv, cache, picked, sources)
 
-    mixed = mixed.reshape(steps, groups, KV_HEADS, width, SHARE, HEAD_DIM)
-    mixed = jnp.transpose(mixed, (0, 1, 3, 2, 4, 5)).reshape(1, steps, part_dev, model)
+    mixed = mixed.reshape(1, steps, part_dev, model)
     return (mixed, forked[None])
 
 

time: 80.2 us -> 77.9 us (0.971)
  Pallas kernels: 65.7 us -> 64 us
    pallas_call x1, Pallas kernels: 65.7 us -> 64 us  [local(): pl.pallas_call(functools.partial(round_kernel, sections, shards, steps, g...]
    transpose x1 -> x0, local copies, waits for them, and re-layouts: 1.64 us -> none  [local(): jnp.transpose(mixed, (0, 1, 3, 2, 4, 5)).reshape(1, steps, part_dev, model)]
    unnamed x8, local copies, waits for them, and re-layouts: 5.14 us -> 6 us
    reshape x2 -> x1, local copies, waits for them, and re-layouts: 2.45 us -> 2.44 us  [local(): mixed = mixed.reshape(1, steps, part_dev, model)]
where the time goes in v3:
time: 77.9 us; the launch traced here: 77.6 us
  Pallas kernels  64 us (82%)
  local copies, waits for them, and re-layouts  9.17 us (12%)
  other arithmetic  3.77 us (5%)
    pallas_call x1, Pallas kernels, local(): pl.pallas_call(functools.partial(round_kernel, sections, shards, steps, g...  64 us
    unnamed x8, local copies, waits for them, and re-layouts  6 us
    reshape x1, local copies, waits for them, and re-layouts, local(): mixed = mixed.reshape(1, steps, part_dev, model)  2.44 us
    concatenate x1, other arithmetic, local(): jnp.concatenate([history_kv[0], jnp.transpose(new_kv[0], (1, 0, 2))], axi...  1.66 us

profile of v3, /device:TPU:5, one launch (start us, length us, event | category | flops | bytes accessed | tf_op | source)
XLA Modules:
  0.0 77.6 jit_solution(11375478713061746133)
XLA Ops:
  0.6 0.0 copy-start.1
  0.6 1.5 %and_select_fusion.source_ref = s32[16]{0:T(128)} fusion(s32[128]{0:T(128)} %param.11, s32[]{:T(128)S(6)} %select_n.27), kind=kLoop, calls=%fused_computation.14 | loop fusion | flops 240 | bytes 132 | tf_op jit(solution)/shard_map/jit(floor_divide)/jit(_where)/select_n | solution.py:274
  2.1 0.7 reshape.18
  2.8 0.7 fusion.2.picked_ref
  3.5 1.2 %copy.14 = bf16[1,4,16,2048]{3,1,2,0:T(4,128)(2,1)S(1)} copy(bf16[1,4,16,2048]{3,2,1,0:T(8,128)(2,1)} %param.10) | data formatting | bytes 524288 | tf_op args[4]
  4.6 2.5 %copy.10 = bf16[8,8,64,128]{3,2,1,0:T(8,128)(2,1)} copy(bf16[8,8,64,128]{3,1,2,0:T(8,128)(2,1)} %bitcast.20) | data formatting | bytes 2097152
  7.1 0.0 copy-done.1
  7.1 1.0 %copy.13 = bf16[1,16,28,2048]{3,2,1,0:T(8,128)(2,1)S(1)} copy(bf16[1,16,28,2048]{3,1,2,0:T(8,128)(2,1)S(1)} %copy-done.1) | data formatting | bytes 3670016 | tf_op args[3]
  8.2 1.7 %pad_maximum_fusion.cache_ref = bf16[16,32,2048]{2,1,0:T(8,128)(2,1)} fusion(bf16[16,4,2048]{2,1,0:T(4,128)(2,1)S(1)} %bitcast.19, bf16[16,28,2048]{2,1,0:T(8,128)(2,1)S(1)} %bitcast.16), kind=kLoop, calls=%fused_computation | loop fusion | flops 4194304 | bytes 4194304 | tf_op jit(solution)/shard_map/concatenate | solution.py:268
  9.8 64.0 %shard_map.77 = (bf16[32,2,64,128]{3,2,1,0:T(8,128)(2,1)}, bf16[16,32,2048]{2,1,0:T(8,128)(2,1)}) custom-call(bf16[32,2,64,128]{3,2,1,0:T(8,128)(2,1)} %bitcast.17, f32[8,8,128]{2,1,0:T(8,128)} %bitcast.21, bf16[1,1024,2048]{2,1,0:T(8,128)(2,1)} %prompt_ref.1, bf16[16,32,2048]{2,1,0:T(8,128)(2,1)} %pad_maximum_fusion.cache_ref, s32[8]{0:T(128)} %fusion.2.picked_ref, ...), custom_call_target="tpu_custom_call" | custom-call | tf_op jit(solution)/shard_map/pallas_call | solution.py:281
  73.8 0.0 copy-start
  73.9 2.4 %reshape.19 = bf16[1,4,16,8192]{3,2,1,0:T(8,128)(2,1)} reshape(bf16[32,2,64,128]{3,2,1,0:T(8,128)(2,1)} %get-tuple-element.4) | data formatting | bytes 2097152 | tf_op jit(solution)/shard_map/reshape | solution.py:321
  76.3 0.0 copy-done
  76.3 1.3 %copy.16 = bf16[1,16,32,2048]{3,2,1,0:T(8,128)(2,1)} copy(bf16[1,16,32,2048]{3,2,1,0:T(8,128)(2,1)S(1)} %bitcast.18) | data formatting | bytes 4194304
Async XLA Ops:
  0.6 6.5 %copy-start.1 = (bf16[1,16,28,2048]{3,1,2,0:T(8,128)(2,1)S(1)}, bf16[1,16,28,2048]{3,1,2,0:T(8,128)(2,1)}, u32[]{:S(2)}) copy-start(bf16[1,16,28,2048]{3,1,2,0:T(8,128)(2,1)} %param.9) | copy-start | bytes 5505028
  73.8 2.5 %copy-start = (bf16[16,32,2048]{2,1,0:T(8,128)(2,1)S(1)}, bf16[16,32,2048]{2,1,0:T(8,128)(2,1)}, u32[]{:S(2)}) copy-start(bf16[16,32,2048]{2,1,0:T(8,128)(2,1)} %get-tuple-element.5) | copy-start | bytes 6291460
